TPU v7x, 512 devices: a whole 4x4x16 slice. The times are simulated.
512 devices in a mesh: dp: 8 (over z_hi, x), tensor: 64 (over z_lo, y, core).
Axes of the slice: x: 4, y: 4, z: 16 (z_hi: 2, z_lo: 8; z = z_hi * 8 + z_lo), core: 2. Of those that a mesh axis runs over, the one named last changes fastest.
Arguments:
- tokens: bfloat16 [4096, 8192], P('dp', 'tensor'), may hold values from -6 to 6
- cotangent: bfloat16 [4096, 8192], P('dp', 'tensor'), may hold values from -6 to 6
- up_first: bfloat16 [64, 256, 128], P('tensor'), may hold values from -0.5 to 0.5
- up_second: bfloat16 [256, 64, 128], P('tensor'), may hold values from -0.75 to 0.75
- down_first: bfloat16 [256, 64, 128], P('tensor'), may hold values from -0.5 to 0.5
- down_second: bfloat16 [64, 256, 128], P('tensor'), may hold values from -0.375 to 0.375
Outputs:
- layer_out: bfloat16 [4096, 8192], P('dp', 'tensor')
- grad_tokens: bfloat16 [4096, 8192], P('dp', 'tensor')
- grad_up_first: float32 [64, 256, 128], P('tensor', 'dp')
- grad_up_second: float32 [256, 64, 128], P('tensor', 'dp')
- grad_down_first: float32 [256, 64, 128], P('tensor', 'dp')
- grad_down_second: float32 [64, 256, 128], P('tensor', 'dp')
All inputs are finite; a program needn't handle non-finite values.
Results may differ from a plain program's by a relative error of at most 0.0061.
Values may be sent and summed in bfloat16 or wider, within the bound.
A program may use at most 64 MiB of HBM per device.

v0:
```python
import jax
import jax.numpy as jnp
from jax import lax
from jax.sharding import PartitionSpec as P


def product(form, left, right):
    return jnp.einsum(form, left, right, preferred_element_type=jnp.float32)


def silu_slope(preact):
    sigma = jax.nn.sigmoid(preact)
    return sigma * (1.0 + preact * (1.0 - sigma))


def hidden_back(back_hidden, preact, down_first, up_second):
    grad_hidden = product("kat,kac->kct", back_hidden, down_first)
    grad_pre = (grad_hidden * silu_slope(preact)).astype(jnp.bfloat16)
    grad_narrow = product("kct,kac->kat", grad_pre, up_second).astype(jnp.bfloat16)
    return (grad_pre, grad_narrow)


def local(tokens, cotangent, up_first, up_second, down_first, down_second):
    tok_rows = tokens.shape[0]
    own_blocks = up_first.shape[0]
    block_width = up_first.shape[2]
    inputs = tokens.reshape(tok_rows, own_blocks, block_width)
    upstream = cotangent.reshape(tok_rows, own_blocks, block_width)
    factor = float(tok_rows * lax.axis_size("dp")) ** (-0.5)
    narrow = product("tab,akb->kat", inputs, up_first).astype(jnp.bfloat16)
    back_narrow = product("tab,akb->kat", upstream, down_second).astype(jnp.bfloat16)
    by_hidden = lax.all_to_all(narrow, "tensor", split_axis=0, concat_axis=1, tiled=True)
    preact = product("kat,kac->kct", by_hidden, up_second)
    hidden = jax.nn.silu(preact).astype(jnp.bfloat16)
    mixed = product("kct,kac->kat", hidden, down_first).astype(jnp.bfloat16)
    mixed_back = lax.all_to_all(mixed, "tensor", split_axis=1, concat_axis=0, tiled=True)
    back_hidden = lax.all_to_all(back_narrow, "tensor", split_axis=0, concat_axis=1, tiled=True)
    grad_pre, grad_narrow = hidden_back(back_hidden, preact, down_first, up_second)
    layer_out = (
        inputs.astype(jnp.float32) + product("kat,akb->tab", mixed_back, down_second)
    ).astype(jnp.bfloat16)
    grad_down_two = product("kat,tab->akb", mixed_back, upstream)
    grad_down_one = product("kat,kct->kac", back_hidden, hidden)
    grad_up_two = product("kat,kct->kac", by_hidden, grad_pre)
    up_back = lax.all_to_all(grad_narrow, "tensor", split_axis=1, concat_axis=0, tiled=True)
    grad_up_one = product("kat,tab->akb", up_back, inputs)
    grad_tokens = (
        upstream.astype(jnp.float32) + product("kat,akb->tab", up_back, up_first)
    ).astype(jnp.bfloat16)
    sum_up_one, sum_up_two, sum_down_one, sum_down_two = (
        lax.psum_scatter(grad_up_one, "dp", scatter_dimension=1, tiled=True),
        lax.psum_scatter(grad_up_two, "dp", scatter_dimension=1, tiled=True),
        lax.psum_scatter(grad_down_one, "dp", scatter_dimension=1, tiled=True),
        lax.psum_scatter(grad_down_two, "dp", scatter_dimension=1, tiled=True),
    )
    return (
        layer_out.reshape(tok_rows, own_blocks * block_width),
        grad_tokens.reshape(tok_rows, own_blocks * block_width),
        sum_up_one * factor,
        sum_up_two * factor,
        sum_down_one * factor,
        sum_down_two * factor,
    )


def solution(mesh):
    placed = (
        P("dp", "tensor"),
        P("dp", "tensor"),
        P("tensor", None, None),
        P("tensor", None, None),
        P("tensor", None, None),
        P("tensor", None, None),
    )
    return jax.shard_map(
        local,
        mesh=mesh,
        in_specs=placed,
        out_specs=(
            P("dp", "tensor"),
            P("dp", "tensor"),
            P("tensor", "dp", None),
            P("tensor", "dp", None),
            P("tensor", "dp", None),
            P("tensor", "dp", None),
        ),
        check_vma=False,
    )
```

profile of v0, /device:TPU:1, one launch (start us, length us, event | category | flops | bytes accessed | tf_op | source)
XLA Modules:
  0.0 533.4 jit_solution(13110442872249819244)
XLA Ops:
  7.2 1.2 fusion.4
  10.6 17.3 %all-to-all-start = ((bf16[64,2,1024]{2,1,0:T(2,128)(2,1)}), bf16[64,2,1024]{2,1,0:T(2,128)(2,1)S(1)}, u32[]{:S(2)}, u32[]{:S(2)}) async-start(bf16[64,2,1024]{2,1,0:T(2,128)(2,1)} %reshape.72), calls=%async_computation | async-start | bytes 524288 | tf_op jit(solution)/shard_map/all_to_all | solution.py:32
  29.8 17.9 %all-to-all-done = bf16[64,2,1024]{2,1,0:T(2,128)(2,1)S(1)} async-done(((bf16[64,2,1024]{2,1,0:T(2,128)(2,1)}), bf16[64,2,1024]{2,1,0:T(2,128)(2,1)S(1)}, u32[]{:S(2)}, u32[]{:S(2)}) %all-to-all-start) | async-done | bytes 262176 | tf_op jit(solution)/shard_map/all_to_all | solution.py:32
  47.8 5.9 %all-to-all-start.2 = ((bf16[64,2,1024]{2,1,0:T(2,128)(2,1)}), bf16[64,2,1024]{2,1,0:T(2,128)(2,1)S(1)}, u32[]{:S(2)}, u32[]{:S(2)}) async-start(bf16[64,2,1024]{2,1,0:T(2,128)(2,1)} %reshape.74), calls=%async_computation.2 | async-start | bytes 524288 | tf_op jit(solution)/shard_map/all_to_all | solution.py:37
  54.0 1.6 reduce
  56.8 0.9 copy.37
  57.7 15.9 %all-to-all-done.2 = bf16[64,2,1024]{2,1,0:T(2,128)(2,1)S(1)} async-done(((bf16[64,2,1024]{2,1,0:T(2,128)(2,1)}), bf16[64,2,1024]{2,1,0:T(2,128)(2,1)S(1)}, u32[]{:S(2)}, u32[]{:S(2)}) %all-to-all-start.2) | async-done | bytes 262176 | tf_op jit(solution)/shard_map/all_to_all | solution.py:37
  73.6 5.9 %all-to-all-start.1 = ((bf16[4,64,512]{2,0,1:T(4,128)(2,1)}), bf16[4,64,512]{2,0,1:T(4,128)(2,1)S(1)}, u32[]{:S(2)}, u32[]{:S(2)}) async-start(bf16[4,64,512]{2,0,1:T(4,128)(2,1)} %copy.37), calls=%async_computation.1 | async-start | bytes 524288 | tf_op jit(solution)/shard_map/all_to_all | solution.py:36
  79.8 1.6 reduce.1
  82.3 0.9 copy.41
  83.2 16.2 %all-to-all-done.1 = bf16[4,64,512]{2,0,1:T(4,128)(2,1)S(1)} async-done(((bf16[4,64,512]{2,0,1:T(4,128)(2,1)}), bf16[4,64,512]{2,0,1:T(4,128)(2,1)S(1)}, u32[]{:S(2)}, u32[]{:S(2)}) %all-to-all-start.1) | async-done | bytes 262176 | tf_op jit(solution)/shard_map/all_to_all | solution.py:36
  99.4 5.9 %all-to-all-start.3 = ((bf16[4,64,512]{2,0,1:T(4,128)(2,1)}), bf16[4,64,512]{2,0,1:T(4,128)(2,1)S(1)}, u32[]{:S(2)}, u32[]{:S(2)}) async-start(bf16[4,64,512]{2,0,1:T(4,128)(2,1)} %copy.41), calls=%async_computation.3 | async-start | bytes 524288 | tf_op jit(solution)/shard_map/all_to_all | solution.py:45
  105.4 0.9 fusion.15
  106.3 0.9 fusion.12
  107.3 108.1 %reduce-scatter.7.cloned.1.call-done = f32[4,8,128]{2,1,0:T(8,128)} async-done(((f32[4,64,128]{2,1,0:T(8,128)}), f32[4,8,128]{2,1,0:T(8,128)}) %reduce-scatter.7.cloned.1.call-update) | async-done | bytes 16400 | tf_op jit(solution)/shard_map/reduce_scatter | solution.py:52
  215.4 1.3 broadcast_multiply_fusion.1
  216.7 102.5 %reduce-scatter.9.cloned.1.call-done = f32[4,8,128]{2,1,0:T(8,128)} async-done(((f32[4,64,128]{2,1,0:T(8,128)}), f32[4,8,128]{2,1,0:T(8,128)}) %reduce-scatter.9.cloned.1.call-update) | async-done | bytes 16400 | tf_op jit(solution)/shard_map/reduce_scatter | solution.py:53
  319.2 1.3 broadcast_multiply_fusion
  323.3 0.9 fusion.11
  324.3 0.9 fusion.10
  325.2 97.3 %reduce-scatter.5.cloned.1.call-done = f32[1,32,128]{2,1,0:T(8,128)} async-done(((f32[1,256,128]{2,1,0:T(8,128)}), f32[1,32,128]{2,1,0:T(8,128)}) %reduce-scatter.5.cloned.1.call-update) | async-done | bytes 16400 | tf_op jit(solution)/shard_map/reduce_scatter | solution.py:51
  422.5 1.3 broadcast_multiply_fusion.3
  423.8 101.8 %reduce-scatter.11.cloned.1.call-done = f32[1,32,128]{2,1,0:T(8,128)} async-done(((f32[1,256,128]{2,1,0:T(8,128)}), f32[1,32,128]{2,1,0:T(8,128)}) %reduce-scatter.11.cloned.1.call-update) | async-done | bytes 16400 | tf_op jit(solution)/shard_map/reduce_scatter | solution.py:54
  525.6 1.3 broadcast_multiply_fusion.2
  (39 shorter events, 9.6 us)
Async XLA Ops:
  7.2 48.4 %copy-start = (bf16[4,64,128]{2,1,0:T(8,128)(2,1)S(1)}, bf16[4,64,128]{2,1,0:T(8,128)(2,1)}, u32[]{:S(2)}) copy-start(bf16[4,64,128]{2,1,0:T(8,128)(2,1)} %param.9) | copy-start | bytes 196612
  10.6 17.4 %copy-start.1 = (bf16[512,128]{1,0:T(8,128)(2,1)S(1)}, bf16[512,128]{1,0:T(8,128)(2,1)}, u32[]{:S(2)}) copy-start(bf16[512,128]{1,0:T(8,128)(2,1)} %param.7) | copy-start | bytes 393220
  10.6 17.4 %copy-start.4 = (bf16[1,256,128]{2,1,0:T(8,128)(2,1)S(1)}, bf16[1,256,128]{2,1,0:T(8,128)(2,1)}, u32[]{:S(2)}) copy-start(bf16[1,256,128]{2,1,0:T(8,128)(2,1)} %param.11) | copy-start | bytes 196612
  10.6 37.2 %all-to-all-start = ((bf16[64,2,1024]{2,1,0:T(2,128)(2,1)}), bf16[64,2,1024]{2,1,0:T(2,128)(2,1)S(1)}, u32[]{:S(2)}, u32[]{:S(2)}) async-start(bf16[64,2,1024]{2,1,0:T(2,128)(2,1)} %reshape.72), calls=%async_computation | async-start | bytes 524288 | tf_op jit(solution)/shard_map/all_to_all | solution.py:32
  47.8 25.8 %all-to-all-start.2 = ((bf16[64,2,1024]{2,1,0:T(2,128)(2,1)}), bf16[64,2,1024]{2,1,0:T(2,128)(2,1)S(1)}, u32[]{:S(2)}, u32[]{:S(2)}) async-start(bf16[64,2,1024]{2,1,0:T(2,128)(2,1)} %reshape.74), calls=%async_computation.2 | async-start | bytes 524288 | tf_op jit(solution)/shard_map/all_to_all | solution.py:37
  55.6 0.8 copy-start.5
  73.6 25.8 %all-to-all-start.1 = ((bf16[4,64,512]{2,0,1:T(4,128)(2,1)}), bf16[4,64,512]{2,0,1:T(4,128)(2,1)S(1)}, u32[]{:S(2)}, u32[]{:S(2)}) async-start(bf16[4,64,512]{2,0,1:T(4,128)(2,1)} %copy.37), calls=%async_computation.1 | async-start | bytes 524288 | tf_op jit(solution)/shard_map/all_to_all | solution.py:36
  99.4 221.2 %all-to-all-start.3 = ((bf16[4,64,512]{2,0,1:T(4,128)(2,1)}), bf16[4,64,512]{2,0,1:T(4,128)(2,1)S(1)}, u32[]{:S(2)}, u32[]{:S(2)}) async-start(bf16[4,64,512]{2,0,1:T(4,128)(2,1)} %copy.41), calls=%async_computation.3 | async-start | bytes 524288 | tf_op jit(solution)/shard_map/all_to_all | solution.py:45
  105.3 110.1 %reduce-scatter.7.cloned.1.call-start = ((), (), s32[]{:S(2)}) async-start(), calls=%async_computation.9 | async-start | bytes 147456 | tf_op jit(solution)/shard_map/reduce_scatter | solution.py:52
  106.3 212.9 %reduce-scatter.9.cloned.1.call-start = ((), (), s32[]{:S(2)}) async-start(), calls=%async_computation.10 | async-start | bytes 147456 | tf_op jit(solution)/shard_map/reduce_scatter | solution.py:53
  107.2 315.3 %reduce-scatter.5.cloned.1.call-start = ((), (), s32[]{:S(2)}) async-start(), calls=%async_computation.8 | async-start | bytes 147456 | tf_op jit(solution)/shard_map/reduce_scatter | solution.py:51
  320.6 0.9 copy-start.2
  322.4 0.9 copy-start.3
  322.4 203.2 %reduce-scatter.11.cloned.1.call-start = ((), (), s32[]{:S(2)}) async-start(), calls=%async_computation.11 | async-start | bytes 147456 | tf_op jit(solution)/shard_map/reduce_scatter | solution.py:54
Sparse Core Ops, SparseCore 0:
  111.1 104.1 reduce-scatter.6
  220.4 98.7 reduce-scatter.8
  323.6 98.8 reduce-scatter.4
  426.8 98.7 reduce-scatter.10
where the time goes:
time: 535 us; the launch traced here: 533 us
  waiting for transfers between devices  460 us (86%)
  starting transfers between devices  35.3 us (7%)
  between operations  14 us (3%)
  other arithmetic  10 us (2%)
  matrix products  8.42 us (2%)
  local copies, waits for them, and re-layouts  5.97 us (1%)
    reduce_scatter x1, waiting for transfers between devices, local(): lax.psum_scatter(grad_up_two, 'dp', scatter_dimension=1, tiled=True)  108 us
    reduce_scatter x1, waiting for transfers between devices, local(): lax.psum_scatter(grad_down_one, 'dp', scatter_dimension=1, tiled=True)  103 us
    reduce_scatter x1, waiting for transfers between devices, local(): lax.psum_scatter(grad_down_two, 'dp', scatter_dimension=1, tiled=True)  102 us
    reduce_scatter x1, waiting for transfers between devices, local(): lax.psum_scatter(grad_up_one, 'dp', scatter_dimension=1, tiled=True)  97.3 us
    all_to_all x1, waiting for transfers between devices, local(): lax.all_to_all(narrow, 'tensor', split_axis=0, concat_axis=1, tiled=True)  17.9 us
    all_to_all x1, starting transfers between devices, local(): lax.all_to_all(narrow, 'tensor', split_axis=0, concat_axis=1, tiled=True)  17.3 us
    all_to_all x1, waiting for transfers between devices, local(): lax.all_to_all(mixed, 'tensor', split_axis=1, concat_axis=0, tiled=True)  16.2 us
    all_to_all x1, waiting for transfers between devices, local(): lax.all_to_all(back_narrow, 'tensor', split_axis=0, concat_axis=1, tiled=...  15.9 us
  transfers between devices with their start and end apart: 8, of which 7 were waited for; matrix products, arithmetic and copies ran while one was open for 3% of the time, Pallas kernels for 0%

commit v1 on v0

v1 whole, which is shorter than its diff:
```python
import functools

import jax
import jax.numpy as jnp
from jax import lax
from jax.experimental import pallas as pl
from jax.experimental.pallas import tpu as pltpu
from jax.sharding import PartitionSpec as P

MESH = pl.DeviceIdType.MESH
F32 = jnp.float32
BF16 = jnp.bfloat16
LANES = 128
ROWS = 16


def dot(left, right, left_dim, right_dim):
    return lax.dot_general(
        left, right, (((left_dim,), (right_dim,)), ((), ())), preferred_element_type=F32
    )


def kernel(
    sizes, factor,
    x_hbm, g_hbm, u1_hbm, u2_hbm, d1_hbm, d2_hbm,
    out_hbm, gt_hbm, gu1_hbm, gu2_hbm, gd1_hbm, gd2_hbm,
    x, g, u1, u2, d1, d2, out, gt, gsum,
    send, recv, wide, nk, bk, hid, slope, gpre,
    part, packed, landed,
    in_sem, out_sem, send_sem, recv_sem, psend_sem, precv_sem,
):
    nt, nd, chunks, kd = sizes
    me = lax.axis_index("tensor")
    my_dp = lax.axis_index("dp")
    hidden_blocks = nt * kd
    tok = chunks * LANES

    barrier = pltpu.get_barrier_semaphore()

    def greet_tensor(j, carry):
        peer = lax.rem(me + j, nt)
        pl.semaphore_signal(barrier, inc=1, device_id={"tensor": peer}, device_id_type=MESH)
        return carry

    def greet_dp(j, carry):
        peer = lax.rem(my_dp + j, nd)
        pl.semaphore_signal(barrier, inc=1, device_id={"dp": peer}, device_id_type=MESH)
        return carry

    lax.fori_loop(1, nt, greet_tensor, 0)
    lax.fori_loop(1, nd, greet_dp, 0)

    loads = [
        pltpu.make_async_copy(src, dst, in_sem.at[i])
        for i, (src, dst) in enumerate(
            ((x_hbm, x), (u1_hbm, u1), (g_hbm, g), (d2_hbm, d2), (u2_hbm, u2), (d1_hbm, d1))
        )
    ]
    for load in loads:
        load.start()

    def exchange(which):
        pltpu.make_async_copy(
            send.at[which, me], recv.at[which, me], recv_sem.at[which]
        ).start()

        def one(j, carry):
            peer = lax.rem(me + j, nt)
            pltpu.make_async_remote_copy(
                src_ref=send.at[which, peer],
                dst_ref=recv.at[which, me],
                send_sem=send_sem.at[which],
                recv_sem=recv_sem.at[which],
                device_id={"tensor": peer},
                device_id_type=MESH,
            ).start()
            return carry

        lax.fori_loop(1, nt, one, 0)

    def arrived(which):
        pltpu.make_async_copy(recv.at[which], recv.at[which], recv_sem.at[which]).wait()

    def narrow_to_send(which, weight, rows):
        for tc in range(chunks):
            wide[which % 2, pl.ds(tc, hidden_blocks, stride=chunks), :] = dot(
                weight[0], rows[tc * LANES:(tc + 1) * LANES, :], 1, 1
            )
        send[which] = wide[which % 2].astype(BF16).reshape(nt, ROWS, LANES)

    def share(which):
        packed[which] = part[which].astype(BF16)

        def one(j, carry):
            peer = lax.rem(my_dp + j, nd)
            pltpu.make_async_remote_copy(
                src_ref=packed.at[which, peer],
                dst_ref=landed.at[which, my_dp],
                send_sem=psend_sem.at[which],
                recv_sem=precv_sem.at[which],
                device_id={"dp": peer},
                device_id_type=MESH,
            ).start()
            return carry

        lax.fori_loop(1, nd, one, 0)

    def reduce(which):
        others = landed.at[which, pl.ds(0, nd - 1)]
        pltpu.make_async_copy(others, others, precv_sem.at[which]).wait()
        total = part[which, my_dp]
        for j in range(1, nd):
            total = total + landed[which, lax.rem(my_dp + j, nd)].astype(F32)
        gsum[which] = total * factor

    loads[0].wait()
    loads[1].wait()
    narrow_to_send(0, u1, x)
    pl.semaphore_wait(barrier, nt + nd - 2)
    exchange(0)
    loads[2].wait()
    loads[3].wait()
    narrow_to_send(1, d2, g)
    exchange(1)
    loads[4].wait()
    loads[5].wait()

    arrived(0)
    wide[0] = recv[0].reshape(nt * ROWS, LANES).astype(F32)
    for k in range(kd):
        for tc in range(chunks):
            nk[k, :, tc * LANES:(tc + 1) * LANES] = wide[
                0, pl.ds(k * chunks + tc, nt, stride=ROWS), :
            ].astype(BF16)
        preact = dot(u2[k], nk[k], 0, 0)
        sigma = 1.0 / (1.0 + jnp.exp(-preact))
        hidden = (preact * sigma).astype(BF16)
        hid[k] = hidden
        slope[k] = sigma * (1.0 + preact * (1.0 - sigma))
        mixed = dot(d1[k], hidden, 1, 0)
        for tc in range(chunks):
            wide[1, pl.ds(k * chunks + tc, nt, stride=ROWS), :] = mixed[
                :, tc * LANES:(tc + 1) * LANES
            ]
    send[2] = wide[1].astype(BF16).reshape(nt, ROWS, LANES)
    exchange(2)

    arrived(1)
    wide[0] = recv[1].reshape(nt * ROWS, LANES).astype(F32)
    for k in range(kd):
        for tc in range(chunks):
            bk[k, :, tc * LANES:(tc + 1) * LANES] = wide[
                0, pl.ds(k * chunks + tc, nt, stride=ROWS), :
            ].astype(BF16)
        grad_pre = (dot(d1[k], bk[k], 0, 0) * slope[k]).astype(BF16)
        gpre[k] = grad_pre
        back = dot(u2[k], grad_pre, 1, 0)
        for tc in range(chunks):
            wide[1, pl.ds(k * chunks + tc, nt, stride=ROWS), :] = back[
                :, tc * LANES:(tc + 1) * LANES
            ]
    send[3] = wide[1].astype(BF16).reshape(nt, ROWS, LANES)
    exchange(3)

    share_rows = nt // nd
    for k in range(kd):
        part[1, :, k * share_rows:(k + 1) * share_rows, :] = dot(bk[k], hid[k], 1, 1).reshape(
            nd, share_rows, LANES
        )
    share(1)
    for k in range(kd):
        part[0, :, k * share_rows:(k + 1) * share_rows, :] = dot(nk[k], gpre[k], 1, 1).reshape(
            nd, share_rows, LANES
        )
    share(0)

    def back_home(which, weight, residual, other, result, slot):
        wide[which % 2] = recv[which].reshape(nt * ROWS, LANES).astype(F32)
        grad = jnp.zeros((hidden_blocks, LANES), F32)
        for tc in range(chunks):
            span = slice(tc * LANES, (tc + 1) * LANES)
            block = wide[which % 2, pl.ds(tc, hidden_blocks, stride=chunks), :].astype(BF16)
            result[span, :] = (
                residual[span, :].astype(F32) + dot(block, weight[0], 0, 0)
            ).astype(BF16)
            grad = grad + dot(block, other[span, :], 1, 0)
        part[slot] = grad.reshape(nd, hidden_blocks // nd, LANES)

    arrived(2)
    back_home(2, d2, x, g, out, 2)
    share(2)
    stores = [pltpu.make_async_copy(out, out_hbm, out_sem.at[0])]
    stores[0].start()
    reduce(1)
    reduce(0)
    for k in range(kd):
        for which, target in ((0, gu2_hbm), (1, gd1_hbm)):
            store = pltpu.make_async_copy(
                gsum.at[which, pl.ds(k * share_rows, share_rows)],
                target.at[k],
                out_sem.at[4 + which * kd + k],
            )
            store.start()
            stores.append(store)

    arrived(3)
    back_home(3, u1, g, x, gt, 3)
    share(3)
    stores.append(pltpu.make_async_copy(gt, gt_hbm, out_sem.at[1]))
    stores[-1].start()
    reduce(2)
    stores.append(pltpu.make_async_copy(gsum.at[2], gd2_hbm.at[0], out_sem.at[2]))
    stores[-1].start()
    reduce(3)
    stores.append(pltpu.make_async_copy(gsum.at[3], gu1_hbm.at[0], out_sem.at[3]))
    stores[-1].start()

    for which in range(4):
        sent = send.at[which, pl.ds(0, nt - 1)]
        pltpu.make_async_copy(sent, sent, send_sem.at[which]).wait()
        sent = packed.at[which, pl.ds(0, nd - 1)]
        pltpu.make_async_copy(sent, sent, psend_sem.at[which]).wait()
    for store in stores:
        store.wait()


def local(tokens, cotangent, up_first, up_second, down_first, down_second):
    nt, nd = lax.axis_size("tensor"), lax.axis_size("dp")
    tok, width = tokens.shape
    kd, blocks, _ = up_second.shape
    hidden_blocks = up_first.shape[1]
    chunks = tok // LANES
    slab = hidden_blocks // nd
    factor = float(tok * nd) ** -0.5
    shapes = (
        jax.ShapeDtypeStruct(tokens.shape, BF16),
        jax.ShapeDtypeStruct(tokens.shape, BF16),
        jax.ShapeDtypeStruct((1, slab, width), F32),
        jax.ShapeDtypeStruct((kd, blocks // nd, LANES), F32),
        jax.ShapeDtypeStruct((kd, blocks // nd, LANES), F32),
        jax.ShapeDtypeStruct((1, slab, width), F32),
    )
    anywhere = pl.BlockSpec(memory_space=pl.ANY)
    return pl.pallas_call(
        functools.partial(kernel, (nt, nd, chunks, kd), factor),
        out_shape=shapes,
        in_specs=[anywhere] * 6,
        out_specs=[anywhere] * 6,
        scratch_shapes=[
            pltpu.VMEM(tokens.shape, BF16),
            pltpu.VMEM(tokens.shape, BF16),
            pltpu.VMEM(up_first.shape, BF16),
            pltpu.VMEM(up_second.shape, BF16),
            pltpu.VMEM(down_first.shape, BF16),
            pltpu.VMEM(down_second.shape, BF16),
            pltpu.VMEM(tokens.shape, BF16),
            pltpu.VMEM(tokens.shape, BF16),
            pltpu.VMEM((4, slab, LANES), F32),
            pltpu.VMEM((4, nt, ROWS, LANES), BF16),
            pltpu.VMEM((4, nt, ROWS, LANES), BF16),
            pltpu.VMEM((2, nt * ROWS, LANES), F32),
            pltpu.VMEM((kd, blocks, tok), BF16),
            pltpu.VMEM((kd, blocks, tok), BF16),
            pltpu.VMEM((kd, LANES, tok), BF16),
            pltpu.VMEM((kd, LANES, tok), F32),
            pltpu.VMEM((kd, LANES, tok), BF16),
            pltpu.VMEM((4, nd, slab, LANES), F32),
            pltpu.VMEM((4, nd, slab, LANES), BF16),
            pltpu.VMEM((4, nd, slab, LANES), BF16),
            pltpu.SemaphoreType.DMA((6,)),
            pltpu.SemaphoreType.DMA((4 + 2 * kd,)),
            pltpu.SemaphoreType.DMA((4,)),
            pltpu.SemaphoreType.DMA((4,)),
            pltpu.SemaphoreType.DMA((4,)),
            pltpu.SemaphoreType.DMA((4,)),
        ],
        compiler_params=pltpu.CompilerParams(
            collective_id=0, has_side_effects=True, vmem_limit_bytes=32 * 1024 * 1024
        ),
        name="monarch",
    )(tokens, cotangent, up_first, up_second, down_first, down_second)


def solution(mesh):
    placed = (
        P("dp", "tensor"),
        P("dp", "tensor"),
        P("tensor", None, None),
        P("tensor", None, None),
        P("tensor", None, None),
        P("tensor", None, None),
    )
    return jax.shard_map(
        local,
        mesh=mesh,
        in_specs=placed,
        out_specs=(
            P("dp", "tensor"),
            P("dp", "tensor"),
            P("tensor", "dp", None),
            P("tensor", "dp", None),
            P("tensor", "dp", None),
            P("tensor", "dp", None),
        ),
        check_vma=False,
    )
```

time: 535 us -> 100 us (0.19)
  the two profiles are of different devices: /device:TPU:1 before, /device:TPU:184 now
where the time goes in v1:
time: 100 us; the launch traced here: 99.9 us
  Pallas kernels  90.3 us (90%)
  local copies, waits for them, and re-layouts  8.89 us (9%)
    pallas_call x1, Pallas kernels, local(): pl.pallas_call(functools.partial(kernel, (nt, nd, chunks, kd), factor), o...  90.3 us
    unnamed x18, local copies, waits for them, and re-layouts  8.89 us

profile of v1, /device:TPU:184, one launch (start us, length us, event | category | flops | bytes accessed | tf_op | source)
XLA Modules:
  0.0 99.9 jit_solution(16731933925250566204)
XLA Ops:
  0.6 0.0 copy-start
  0.6 0.9 copy-done
  1.5 0.0 copy-start.1
  1.5 0.9 copy-done.1
  2.4 0.0 copy-start.2
  2.4 0.8 copy-done.2
  3.3 0.0 copy-start.3
  3.3 0.8 copy-done.3
  4.1 0.0 copy-start.4
  4.1 0.8 copy-done.4
  5.0 0.0 copy-start.5
  5.0 0.8 copy-done.5
  5.8 90.3 %monarch.1 = (bf16[512,128]{1,0:T(8,128)(2,1)S(1)}, bf16[512,128]{1,0:T(8,128)(2,1)S(1)}, f32[1,32,128]{2,1,0:T(8,128)S(1)}, f32[4,8,128]{2,1,0:T(8,128)S(1)}, f...) custom-call(bf16[512,128]{1,0:T(8,128)(2,1)S(1)} %copy-done, bf16[512,128]{1,0:T(8,128)(2,1)S(1)} %copy-done.1, ...), custom_call_target="tpu_custom_call" | custom-call | tf_op jit(solution)/shard_map/monarch/pallas_call | solution.py:244
  96.1 0.7 copy.18
  96.8 0.7 copy.19
  97.4 0.6 copy.20
  98.1 0.6 copy.21
  98.7 0.6 copy.22
  99.3 0.6 copy.23
Async XLA Ops:
  0.6 0.9 copy-start
  1.5 0.9 copy-start.1
  2.4 0.8 copy-start.2
  3.3 0.8 copy-start.3
  4.1 0.8 copy-start.4
  5.0 0.8 copy-start.5

commit v2 on v1

--- a/solution.py
+++ b/solution.py
@@ -23,15 +23,20 @@
 def kernel(
     sizes, factor,
     x_hbm, g_hbm, u1_hbm, u2_hbm, d1_hbm, d2_hbm,
-    out_hbm, gt_hbm, gu1_hbm, gu2_hbm, gd1_hbm, gd2_hbm,
-    x, g, u1, u2, d1, d2, out, gt, gsum,
+    out, gt, gu1, gu2, gd1, gd2,
+    x, g, u1, u2, d1, d2,
     send, recv, wide, nk, bk, hid, slope, gpre,
-    part, packed, landed,
-    in_sem, out_sem, send_sem, recv_sem, psend_sem, precv_sem,
+    part, packed, landed, half, half_packed, half_landed,
+    in_sem, send_sem, recv_sem, psend_sem, precv_sem, hsend_sem, hrecv_sem,
 ):
     nt, nd, chunks, kd = sizes
+    nx = nd // 2
     me = lax.axis_index("tensor")
     my_dp = lax.axis_index("dp")
+    my_half = my_dp // nx
+    my_x = lax.rem(my_dp, nx)
+    other_half = 1 - my_half
+    partner = other_half * nx + my_x
     hidden_blocks = nt * kd
     tok = chunks * LANES
 
@@ -42,13 +47,15 @@
         pl.semaphore_signal(barrier, inc=1, device_id={"tensor": peer}, device_id_type=MESH)
         return carry
 
-    def greet_dp(j, carry):
-        peer = lax.rem(my_dp + j, nd)
-        pl.semaphore_signal(barrier, inc=1, device_id={"dp": peer}, device_id_type=MESH)
-        return carry
-
+    def x_peer(j):
+        return lax.rem(my_x + j, nx)
+
+    pl.semaphore_signal(barrier, inc=1, device_id={"dp": partner}, device_id_type=MESH)
     lax.fori_loop(1, nt, greet_tensor, 0)
-    lax.fori_loop(1, nd, greet_dp, 0)
+    for j in range(1, nx):
+        pl.semaphore_signal(
+            barrier, inc=1, device_id={"dp": my_half * nx + x_peer(j)}, device_id_type=MESH
+        )
 
     loads = [
         pltpu.make_async_copy(src, dst, in_sem.at[i])
@@ -90,33 +97,49 @@
 
     def share(which):
         packed[which] = part[which].astype(BF16)
-
-        def one(j, carry):
-            peer = lax.rem(my_dp + j, nd)
+        for j in range(1, nx):
             pltpu.make_async_remote_copy(
-                src_ref=packed.at[which, peer],
-                dst_ref=landed.at[which, my_dp],
+                src_ref=packed.at[which, :, x_peer(j)],
+                dst_ref=landed.at[which, my_x],
                 send_sem=psend_sem.at[which],
                 recv_sem=precv_sem.at[which],
-                device_id={"dp": peer},
+                device_id={"dp": my_half * nx + x_peer(j)},
                 device_id_type=MESH,
             ).start()
-            return carry
-
-        lax.fori_loop(1, nd, one, 0)
-
-    def reduce(which):
-        others = landed.at[which, pl.ds(0, nd - 1)]
+
+    def hand_over(which):
+        others = landed.at[which, pl.ds(0, nx - 1)]
         pltpu.make_async_copy(others, others, precv_sem.at[which]).wait()
-        total = part[which, my_dp]
-        for j in range(1, nd):
-            total = total + landed[which, lax.rem(my_dp + j, nd)].astype(F32)
-        gsum[which] = total * factor
+
+        def total(side):
+            value = part[which, side, my_x]
+            for j in range(1, nx):
+                value = value + landed[which, x_peer(j), side].astype(F32)
+            return value
+
+        half_packed[which] = total(other_half).astype(BF16)
+        across(which).start()
+        half[which] = total(my_half)
+
+    def across(which):
+        return pltpu.make_async_remote_copy(
+            src_ref=half_packed.at[which],
+            dst_ref=half_landed.at[which],
+            send_sem=hsend_sem.at[which],
+            recv_sem=hrecv_sem.at[which],
+            device_id={"dp": partner},
+            device_id_type=MESH,
+        )
+
+    def finish(which, target):
+        across(which).wait_recv()
+        value = (half[which] + half_landed[which].astype(F32)) * factor
+        target[...] = value.reshape(target.shape)
 
     loads[0].wait()
     loads[1].wait()
     narrow_to_send(0, u1, x)
-    pl.semaphore_wait(barrier, nt + nd - 2)
+    pl.semaphore_wait(barrier, nt - 1 + nx)
     exchange(0)
     loads[2].wait()
     loads[3].wait()
@@ -164,13 +187,13 @@
 
     share_rows = nt // nd
     for k in range(kd):
-        part[1, :, k * share_rows:(k + 1) * share_rows, :] = dot(bk[k], hid[k], 1, 1).reshape(
-            nd, share_rows, LANES
+        part[1, :, :, k * share_rows:(k + 1) * share_rows, :] = dot(bk[k], hid[k], 1, 1).reshape(
+            2, nx, share_rows, LANES
         )
     share(1)
     for k in range(kd):
-        part[0, :, k * share_rows:(k + 1) * share_rows, :] = dot(nk[k], gpre[k], 1, 1).reshape(
-            nd, share_rows, LANES
+        part[0, :, :, k * share_rows:(k + 1) * share_rows, :] = dot(nk[k], gpre[k], 1, 1).reshape(
+            2, nx, share_rows, LANES
         )
     share(0)
 
@@ -184,44 +207,42 @@
                 residual[span, :].astype(F32) + dot(block, weight[0], 0, 0)
             ).astype(BF16)
             grad = grad + dot(block, other[span, :], 1, 0)
-        part[slot] = grad.reshape(nd, hidden_blocks // nd, LANES)
+        part[slot] = grad.reshape(2, nx, hidden_blocks // nd, LANES)
 
     arrived(2)
     back_home(2, d2, x, g, out, 2)
     share(2)
-    stores = [pltpu.make_async_copy(out, out_hbm, out_sem.at[0])]
-    stores[0].start()
-    reduce(1)
-    reduce(0)
-    for k in range(kd):
-        for which, target in ((0, gu2_hbm), (1, gd1_hbm)):
-            store = pltpu.make_async_copy(
-                gsum.at[which, pl.ds(k * share_rows, share_rows)],
-                target.at[k],
-                out_sem.at[4 + which * kd + k],
-            )
-            store.start()
-            stores.append(store)
+    hand_over(1)
+    hand_over(0)
+    hand_over(2)
+    finish(1, gd1)
+    finish(0, gu2)
 
     arrived(3)
     back_home(3, u1, g, x, gt, 3)
     share(3)
-    stores.append(pltpu.make_async_copy(gt, gt_hbm, out_sem.at[1]))
-    stores[-1].start()
-    reduce(2)
-    stores.append(pltpu.make_async_copy(gsum.at[2], gd2_hbm.at[0], out_sem.at[2]))
-    stores[-1].start()
-    reduce(3)
-    stores.append(pltpu.make_async_copy(gsum.at[3], gu1_hbm.at[0], out_sem.at[3]))
-    stores[-1].start()
+    finish(2, gd2)
+    hand_over(3)
+    finish(3, gu1)
 
     for which in range(4):
         sent = send.at[which, pl.ds(0, nt - 1)]
         pltpu.make_async_copy(sent, sent, send_sem.at[which]).wait()
-        sent = packed.at[which, pl.ds(0, nd - 1)]
+        sent = packed.at[which, :, pl.ds(0, nx - 1)]
         pltpu.make_async_copy(sent, sent, psend_sem.at[which]).wait()
-    for store in stores:
-        store.wait()
+        across(which).wait_send()
+
+
+def write_out(*refs):
+    count = len(refs) // 2
+    sems = refs[-1]
+    copies = [
+        pltpu.make_async_copy(refs[i], refs[count + i], sems.at[i]) for i in range(count)
+    ]
+    for copy in copies:
+        copy.start()
+    for copy in copies:
+        copy.wait()
 
 
 def local(tokens, cotangent, up_first, up_second, down_first, down_second):
@@ -240,12 +261,13 @@
         jax.ShapeDtypeStruct((kd, blocks // nd, LANES), F32),
         jax.ShapeDtypeStruct((1, slab, width), F32),
     )
-    anywhere = pl.BlockSpec(memory_space=pl.ANY)
-    return pl.pallas_call(
+    in_hbm = pl.BlockSpec(memory_space=pltpu.HBM)
+    in_vmem = pl.BlockSpec(memory_space=pltpu.VMEM)
+    results = pl.pallas_call(
         functools.partial(kernel, (nt, nd, chunks, kd), factor),
         out_shape=shapes,
-        in_specs=[anywhere] * 6,
-        out_specs=[anywhere] * 6,
+        in_specs=[in_hbm] * 6,
+        out_specs=[in_vmem] * 6,
         scratch_shapes=[
             pltpu.VMEM(tokens.shape, BF16),
             pltpu.VMEM(tokens.shape, BF16),
@@ -253,9 +275,6 @@
             pltpu.VMEM(up_second.shape, BF16),
             pltpu.VMEM(down_first.shape, BF16),
             pltpu.VMEM(down_second.shape, BF16),
-            pltpu.VMEM(tokens.shape, BF16),
-            pltpu.VMEM(tokens.shape, BF16),
-            pltpu.VMEM((4, slab, LANES), F32),
             pltpu.VMEM((4, nt, ROWS, LANES), BF16),
             pltpu.VMEM((4, nt, ROWS, LANES), BF16),
             pltpu.VMEM((2, nt * ROWS, LANES), F32),
@@ -264,21 +283,33 @@
             pltpu.VMEM((kd, LANES, tok), BF16),
             pltpu.VMEM((kd, LANES, tok), F32),
             pltpu.VMEM((kd, LANES, tok), BF16),
-            pltpu.VMEM((4, nd, slab, LANES), F32),
-            pltpu.VMEM((4, nd, slab, LANES), BF16),
-            pltpu.VMEM((4, nd, slab, LANES), BF16),
+            pltpu.VMEM((4, 2, nd // 2, slab, LANES), F32),
+            pltpu.VMEM((4, 2, nd // 2, slab, LANES), BF16),
+            pltpu.VMEM((4, nd // 2, 2, slab, LANES), BF16),
+            pltpu.VMEM((4, slab, LANES), F32),
+            pltpu.VMEM((4, slab, LANES), BF16),
+            pltpu.VMEM((4, slab, LANES), BF16),
             pltpu.SemaphoreType.DMA((6,)),
-            pltpu.SemaphoreType.DMA((4 + 2 * kd,)),
+            pltpu.SemaphoreType.DMA((4,)),
+            pltpu.SemaphoreType.DMA((4,)),
             pltpu.SemaphoreType.DMA((4,)),
             pltpu.SemaphoreType.DMA((4,)),
             pltpu.SemaphoreType.DMA((4,)),
             pltpu.SemaphoreType.DMA((4,)),
         ],
         compiler_params=pltpu.CompilerParams(
-            collective_id=0, has_side_effects=True, vmem_limit_bytes=32 * 1024 * 1024
+            collective_id=0, has_side_effects=True, vmem_limit_bytes=63 * 1024 * 1024
         ),
         name="monarch",
     )(tokens, cotangent, up_first, up_second, down_first, down_second)
+    return pl.pallas_call(
+        write_out,
+        out_shape=shapes,
+        in_specs=[in_vmem] * 6,
+        out_specs=[in_hbm] * 6,
+        scratch_shapes=[pltpu.SemaphoreType.DMA((6,))],
+        name="write_out",
+    )(*results)
 
 
 def solution(mesh):

time: 100 us -> 82.9 us (0.83)
  local copies, waits for them, and re-layouts: 8.89 us -> 0 us
  Pallas kernels: 90.3 us -> 82.1 us
    pallas_call x1, Pallas kernels: 90.3 us -> 80.4 us  [local(): pl.pallas_call(functools.partial(kernel, (nt, nd, chunks, kd), factor), o...]
    unnamed x18 -> x0, local copies, waits for them, and re-layouts: 8.89 us -> none
    pallas_call x0 -> x1, Pallas kernels: none -> 1.75 us  [local(): pl.pallas_call(write_out, out_shape=shapes, in_specs=[in_vmem] * 6, out_s...]
where the time goes in v2:
time: 82.9 us; the launch traced here: 82.8 us
  Pallas kernels  82.1 us (99%)
    pallas_call x1, Pallas kernels, local(): pl.pallas_call(functools.partial(kernel, (nt, nd, chunks, kd), factor), o...  80.4 us
    pallas_call x1, Pallas kernels, local(): pl.pallas_call(write_out, out_shape=shapes, in_specs=[in_vmem] * 6, out_s...  1.75 us

profile of v2, /device:TPU:184, one launch (start us, length us, event | category | flops | bytes accessed | tf_op | source)
XLA Modules:
  0.0 82.8 jit_solution(1287837250035549864)
XLA Ops:
  0.6 80.4 %monarch.1 = (bf16[512,128]{1,0:T(8,128)(2,1)}, bf16[512,128]{1,0:T(8,128)(2,1)}, f32[1,32,128]{2,1,0:T(8,128)}, f32[4,8,128]{2,1,0:T(8,128)}, f32[4,8,128]{2,1,0:T(8,128)}, /*index=5*/f32[1,32,128]{2,1,0:T(8,128)}) custom-call(bf16[512,128]{1,0:T(8,128)(2,1)} %x_hbm.1, bf16[512,128]{1,0:T(8,128)(2,1)} %g_hbm.1, bf16[1,256,128]{2,1,0:T(8,128)(2,1)} %u1_hbm.1, ...), custom_call_target="tpu_custom_call" | custom-call | tf_op jit(solution)/shard_map/monarch/pallas_call | solution.py:266
  81.0 1.8 %write_out.1 = (bf16[512,128]{1,0:T(8,128)(2,1)}, bf16[512,128]{1,0:T(8,128)(2,1)}, f32[1,32,128]{2,1,0:T(8,128)}, f32[4,8,128]{2,1,0:T(8,128)}, f32[4,8,128]{2,1,0:T(8,128)}, /*index=5*/f32[1,32,128]{2,1,0:T(8,128)}) custom-call(bf16[512,128]{1,0:T(8,128)(2,1)} %get-tuple-element.12.refs_0_, bf16[512,128]{1,0:T(8,128)(2,1)} %get-tuple-element.13.refs_1_, ...), custom_call_target="tpu_custom_call" | custom-call | tf_op jit(solution)/shard_map/write_out/pallas_call | solution.py:305

commit v3 on v2

--- a/solution.py
+++ b/solution.py
@@ -26,7 +26,7 @@
     out, gt, gu1, gu2, gd1, gd2,
     x, g, u1, u2, d1, d2,
     send, recv, wide, nk, bk, hid, slope, gpre,
-    part, packed, landed, half, half_packed, half_landed,
+    home, part, packed, landed, half, half_packed, half_landed,
     in_sem, send_sem, recv_sem, psend_sem, precv_sem, hsend_sem, hrecv_sem,
 ):
     nt, nd, chunks, kd = sizes
@@ -41,9 +41,13 @@
     tok = chunks * LANES
 
     barrier = pltpu.get_barrier_semaphore()
+    step = jnp.where(me >= nt // 2, 1, -1)
+
+    def tensor_peer(j):
+        return lax.rem(me + nt + step * j, nt)
 
     def greet_tensor(j, carry):
-        peer = lax.rem(me + j, nt)
+        peer = tensor_peer(j)
         pl.semaphore_signal(barrier, inc=1, device_id={"tensor": peer}, device_id_type=MESH)
         return carry
 
@@ -72,7 +76,7 @@
         ).start()
 
         def one(j, carry):
-            peer = lax.rem(me + j, nt)
+            peer = tensor_peer(j)
             pltpu.make_async_remote_copy(
                 src_ref=send.at[which, peer],
                 dst_ref=recv.at[which, me],
@@ -197,32 +201,44 @@
         )
     share(0)
 
-    def back_home(which, weight, residual, other, result, slot):
+    def unpack(which):
         wide[which % 2] = recv[which].reshape(nt * ROWS, LANES).astype(F32)
+        for tc in range(chunks):
+            home[which % 2, tc] = wide[
+                which % 2, pl.ds(tc, hidden_blocks, stride=chunks), :
+            ].astype(BF16)
+
+    def factor_grad(which, other):
         grad = jnp.zeros((hidden_blocks, LANES), F32)
         for tc in range(chunks):
+            grad = grad + dot(home[which % 2, tc], other[tc * LANES:(tc + 1) * LANES, :], 1, 0)
+        part[which] = grad.reshape(2, nx, hidden_blocks // nd, LANES)
+
+    def leave(which, weight, residual, result):
+        for tc in range(chunks):
             span = slice(tc * LANES, (tc + 1) * LANES)
-            block = wide[which % 2, pl.ds(tc, hidden_blocks, stride=chunks), :].astype(BF16)
             result[span, :] = (
-                residual[span, :].astype(F32) + dot(block, weight[0], 0, 0)
+                residual[span, :].astype(F32) + dot(home[which % 2, tc], weight[0], 0, 0)
             ).astype(BF16)
-            grad = grad + dot(block, other[span, :], 1, 0)
-        part[slot] = grad.reshape(2, nx, hidden_blocks // nd, LANES)
 
     arrived(2)
-    back_home(2, d2, x, g, out, 2)
+    unpack(2)
+    factor_grad(2, g)
     share(2)
+    leave(2, d2, x, out)
+
+    arrived(3)
+    unpack(3)
+    factor_grad(3, x)
+    share(3)
     hand_over(1)
     hand_over(0)
     hand_over(2)
+    leave(3, u1, g, gt)
+    hand_over(3)
     finish(1, gd1)
     finish(0, gu2)
-
-    arrived(3)
-    back_home(3, u1, g, x, gt, 3)
-    share(3)
     finish(2, gd2)
-    hand_over(3)
     finish(3, gu1)
 
     for which in range(4):
@@ -261,8 +277,8 @@
         jax.ShapeDtypeStruct((kd, blocks // nd, LANES), F32),
         jax.ShapeDtypeStruct((1, slab, width), F32),
     )
+    in_vmem = pl.BlockSpec(memory_space=pltpu.VMEM)
     in_hbm = pl.BlockSpec(memory_space=pltpu.HBM)
-    in_vmem = pl.BlockSpec(memory_space=pltpu.VMEM)
     results = pl.pallas_call(
         functools.partial(kernel, (nt, nd, chunks, kd), factor),
         out_shape=shapes,
@@ -283,6 +299,7 @@
             pltpu.VMEM((kd, LANES, tok), BF16),
             pltpu.VMEM((kd, LANES, tok), F32),
             pltpu.VMEM((kd, LANES, tok), BF16),
+            pltpu.VMEM((2, chunks, hidden_blocks, LANES), BF16),
             pltpu.VMEM((4, 2, nd // 2, slab, LANES), F32),
             pltpu.VMEM((4, 2, nd // 2, slab, LANES), BF16),
             pltpu.VMEM((4, nd // 2, 2, slab, LANES), BF16),

time: 82.9 us -> 78.3 us (0.945)
  the two profiles are of different devices: /device:TPU:184 before, /device:TPU:1 now
where the time goes in v3:
time: 78.3 us; the launch traced here: 77.7 us
  Pallas kernels  77.1 us (98%)
    pallas_call x1, Pallas kernels, local(): pl.pallas_call(functools.partial(kernel, (nt, nd, chunks, kd), factor), o...  75.3 us
    pallas_call x1, Pallas kernels, local(): pl.pallas_call(write_out, out_shape=shapes, in_specs=[in_vmem] * 6, out_s...  1.75 us

profile of v3, /device:TPU:1, one launch (start us, length us, event | category | flops | bytes accessed | tf_op | source)
XLA Modules:
  0.0 77.7 jit_solution(3623485946964743000)
XLA Ops:
  0.6 75.3 %monarch.1 = (bf16[512,128]{1,0:T(8,128)(2,1)}, bf16[512,128]{1,0:T(8,128)(2,1)}, f32[1,32,128]{2,1,0:T(8,128)}, f32[4,8,128]{2,1,0:T(8,128)}, f32[4,8,128]{2,1,0:T(8,128)}, /*index=5*/f32[1,32,128]{2,1,0:T(8,128)}) custom-call(bf16[512,128]{1,0:T(8,128)(2,1)} %x_hbm.1, bf16[512,128]{1,0:T(8,128)(2,1)} %g_hbm.1, bf16[1,256,128]{2,1,0:T(8,128)(2,1)} %u1_hbm.1, ...), custom_call_target="tpu_custom_call" | custom-call | tf_op jit(solution)/shard_map/monarch/pallas_call | solution.py:282
  76.0 1.8 %write_out.1 = (bf16[512,128]{1,0:T(8,128)(2,1)}, bf16[512,128]{1,0:T(8,128)(2,1)}, f32[1,32,128]{2,1,0:T(8,128)}, f32[4,8,128]{2,1,0:T(8,128)}, f32[4,8,128]{2,1,0:T(8,128)}, /*index=5*/f32[1,32,128]{2,1,0:T(8,128)}) custom-call(bf16[512,128]{1,0:T(8,128)(2,1)} %get-tuple-element.12.refs_0_, bf16[512,128]{1,0:T(8,128)(2,1)} %get-tuple-element.13.refs_1_, ...), custom_call_target="tpu_custom_call" | custom-call | tf_op jit(solution)/shard_map/write_out/pallas_call | solution.py:322

commit v4 on v3

--- a/solution.py
+++ b/solution.py
@@ -23,11 +23,11 @@
 def kernel(
     sizes, factor,
     x_hbm, g_hbm, u1_hbm, u2_hbm, d1_hbm, d2_hbm,
-    out, gt, gu1, gu2, gd1, gd2,
-    x, g, u1, u2, d1, d2,
+    out_hbm, gt_hbm, gu1_hbm, gu2_hbm, gd1_hbm, gd2_hbm,
+    x, g, u1, u2, d1, d2, out, gt, gsum,
     send, recv, wide, nk, bk, hid, slope, gpre,
-    home, part, packed, landed, half, half_packed, half_landed,
-    in_sem, send_sem, recv_sem, psend_sem, precv_sem, hsend_sem, hrecv_sem,
+    home, part, packed, landed, direct, half, half_packed, half_landed,
+    in_sem, out_sem, send_sem, recv_sem, psend_sem, precv_sem, hsend_sem, hrecv_sem,
 ):
     nt, nd, chunks, kd = sizes
     nx = nd // 2
@@ -37,6 +37,8 @@
     my_x = lax.rem(my_dp, nx)
     other_half = 1 - my_half
     partner = other_half * nx + my_x
+    run_half = me // (nt // 2)
+    sides = (run_half, 1 - run_half)
     hidden_blocks = nt * kd
     tok = chunks * LANES
 
@@ -54,7 +56,10 @@
     def x_peer(j):
         return lax.rem(my_x + j, nx)
 
-    pl.semaphore_signal(barrier, inc=1, device_id={"dp": partner}, device_id_type=MESH)
+    for j in range(nx):
+        pl.semaphore_signal(
+            barrier, inc=1, device_id={"dp": other_half * nx + x_peer(j)}, device_id_type=MESH
+        )
     lax.fori_loop(1, nt, greet_tensor, 0)
     for j in range(1, nx):
         pl.semaphore_signal(
@@ -77,11 +82,12 @@
 
         def one(j, carry):
             peer = tensor_peer(j)
+            side = lax.rem(peer // (nt // 2) + run_half, 2) if which == 3 else 0
             pltpu.make_async_remote_copy(
                 src_ref=send.at[which, peer],
                 dst_ref=recv.at[which, me],
                 send_sem=send_sem.at[which],
-                recv_sem=recv_sem.at[which],
+                recv_sem=recv_sem.at[which + side],
                 device_id={"tensor": peer},
                 device_id_type=MESH,
             ).start()
@@ -135,15 +141,33 @@
             device_id_type=MESH,
         )
 
-    def finish(which, target):
+    def finish(which):
         across(which).wait_recv()
-        value = (half[which] + half_landed[which].astype(F32)) * factor
-        target[...] = value.reshape(target.shape)
+        gsum[which] = (half[which] + half_landed[which].astype(F32)) * factor
+
+    def finish_direct():
+        others = direct.at[pl.ds(0, nd - 1)]
+        pltpu.make_async_copy(others, others, precv_sem.at[3]).wait()
+        value = part[3, my_half, my_x]
+        for j in range(1, nd):
+            value = value + direct[lax.rem(my_dp + j, nd)].astype(F32)
+        gsum[3] = value * factor
+
+    stores = []
+
+    def store(src, dst):
+        copy = pltpu.make_async_copy(src, dst, out_sem.at[len(stores)])
+        copy.start()
+        stores.append(copy)
+
+    def store_sum(which, target):
+        for k in range(kd):
+            store(gsum.at[which, pl.ds(k * share_rows, share_rows)], target.at[k])
 
     loads[0].wait()
     loads[1].wait()
     narrow_to_send(0, u1, x)
-    pl.semaphore_wait(barrier, nt - 1 + nx)
+    pl.semaphore_wait(barrier, nt - 1 + nd - 1)
     exchange(0)
     loads[2].wait()
     loads[3].wait()
@@ -221,32 +245,87 @@
                 residual[span, :].astype(F32) + dot(home[which % 2, tc], weight[0], 0, 0)
             ).astype(BF16)
 
+    def arrived_side(side):
+        block = recv.at[3, pl.ds(sides[side] * (nt // 2), nt // 2)]
+        pltpu.make_async_copy(block, block, recv_sem.at[3 + side]).wait()
+
+    def unpack_side(side):
+        count = nt * ROWS // 2
+        block = recv[3, pl.ds(sides[side] * (nt // 2), nt // 2)]
+        wide[1, side * count:(side + 1) * count, :] = block.reshape(count, LANES).astype(F32)
+        for tc in range(chunks):
+            home[1, tc, side_rows(side), :] = wide[
+                1, pl.ds(side * count + tc, hidden_blocks // 2, stride=chunks), :
+            ].astype(BF16)
+
+    def side_rows(side):
+        return slice(side * hidden_blocks // 2, (side + 1) * hidden_blocks // 2)
+
+    def share_side(side):
+        target = sides[side]
+        grad = jnp.zeros((hidden_blocks // 2, LANES), F32)
+        for tc in range(chunks):
+            span = slice(tc * LANES, (tc + 1) * LANES)
+            grad = grad + dot(home[1, tc, side_rows(side), :], x[span, :], 1, 0)
+        grad = grad.reshape(nx, hidden_blocks // nd, LANES)
+        part[3, target] = grad
+        packed[3, target] = grad.astype(BF16)
+        for j in range(nx):
+            copy = pltpu.make_async_remote_copy(
+                src_ref=packed.at[3, target, x_peer(j)],
+                dst_ref=direct.at[my_dp],
+                send_sem=psend_sem.at[3],
+                recv_sem=precv_sem.at[3],
+                device_id={"dp": target * nx + x_peer(j)},
+                device_id_type=MESH,
+            )
+            if j > 0:
+                copy.start()
+            else:
+                pl.when(target != my_half)(copy.start)
+
     arrived(2)
     unpack(2)
     factor_grad(2, g)
     share(2)
     leave(2, d2, x, out)
-
-    arrived(3)
-    unpack(3)
-    factor_grad(3, x)
-    share(3)
+    store(out, out_hbm)
+
+    for side in range(2):
+        arrived_side(side)
+        unpack_side(side)
+        share_side(side)
     hand_over(1)
     hand_over(0)
     hand_over(2)
-    leave(3, u1, g, gt)
-    hand_over(3)
-    finish(1, gd1)
-    finish(0, gu2)
-    finish(2, gd2)
-    finish(3, gu1)
+    for tc in range(chunks):
+        span = slice(tc * LANES, (tc + 1) * LANES)
+        value = g[span, :].astype(F32)
+        for side in range(2):
+            rows = pl.ds(sides[side] * (hidden_blocks // 2), hidden_blocks // 2)
+            value = value + dot(home[1, tc, side_rows(side), :], u1[0, rows, :], 0, 0)
+        gt[span, :] = value.astype(BF16)
+    store(gt, gt_hbm)
+    finish(1)
+    store_sum(1, gd1_hbm)
+    finish(0)
+    store_sum(0, gu2_hbm)
+    finish(2)
+    store(gsum.at[2], gd2_hbm.at[0])
+    finish_direct()
+    store(gsum.at[3], gu1_hbm.at[0])
 
     for which in range(4):
         sent = send.at[which, pl.ds(0, nt - 1)]
         pltpu.make_async_copy(sent, sent, send_sem.at[which]).wait()
+    for which in range(3):
         sent = packed.at[which, :, pl.ds(0, nx - 1)]
         pltpu.make_async_copy(sent, sent, psend_sem.at[which]).wait()
         across(which).wait_send()
+    sent = direct.at[pl.ds(0, nd - 1)]
+    pltpu.make_async_copy(sent, sent, psend_sem.at[3]).wait()
+    for copy in stores:
+        copy.wait()
 
 
 def write_out(*refs):
@@ -283,7 +362,7 @@
         functools.partial(kernel, (nt, nd, chunks, kd), factor),
         out_shape=shapes,
         in_specs=[in_hbm] * 6,
-        out_specs=[in_vmem] * 6,
+        out_specs=[in_hbm] * 6,
         scratch_shapes=[
             pltpu.VMEM(tokens.shape, BF16),
             pltpu.VMEM(tokens.shape, BF16),
@@ -291,6 +370,9 @@
             pltpu.VMEM(up_second.shape, BF16),
             pltpu.VMEM(down_first.shape, BF16),
             pltpu.VMEM(down_second.shape, BF16),
+            pltpu.VMEM(tokens.shape, BF16),
+            pltpu.VMEM(tokens.shape, BF16),
+            pltpu.VMEM((4, slab, LANES), F32),
             pltpu.VMEM((4, nt, ROWS, LANES), BF16),
             pltpu.VMEM((4, nt, ROWS, LANES), BF16),
             pltpu.VMEM((2, nt * ROWS, LANES), F32),
@@ -302,17 +384,19 @@
             pltpu.VMEM((2, chunks, hidden_blocks, LANES), BF16),
             pltpu.VMEM((4, 2, nd // 2, slab, LANES), F32),
             pltpu.VMEM((4, 2, nd // 2, slab, LANES), BF16),
-            pltpu.VMEM((4, nd // 2, 2, slab, LANES), BF16),
-            pltpu.VMEM((4, slab, LANES), F32),
-            pltpu.VMEM((4, slab, LANES), BF16),
-            pltpu.VMEM((4, slab, LANES), BF16),
+            pltpu.VMEM((3, nd // 2, 2, slab, LANES), BF16),
+            pltpu.VMEM((nd, slab, LANES), BF16),
+            pltpu.VMEM((3, slab, LANES), F32),
+            pltpu.VMEM((3, slab, LANES), BF16),
+            pltpu.VMEM((3, slab, LANES), BF16),
             pltpu.SemaphoreType.DMA((6,)),
+            pltpu.SemaphoreType.DMA((4 + 2 * kd,)),
+            pltpu.SemaphoreType.DMA((4,)),
+            pltpu.SemaphoreType.DMA((5,)),
             pltpu.SemaphoreType.DMA((4,)),
             pltpu.SemaphoreType.DMA((4,)),
-            pltpu.SemaphoreType.DMA((4,)),
-            pltpu.SemaphoreType.DMA((4,)),
-            pltpu.SemaphoreType.DMA((4,)),
-            pltpu.SemaphoreType.DMA((4,)),
+            pltpu.SemaphoreType.DMA((3,)),
+            pltpu.SemaphoreType.DMA((3,)),
         ],
         compiler_params=pltpu.CompilerParams(
             collective_id=0, has_side_effects=True, vmem_limit_bytes=63 * 1024 * 1024

time: 78.3 us -> 76.5 us (0.977)
  Pallas kernels: 77.1 us -> 75.7 us
    pallas_call x1, Pallas kernels: 75.3 us -> 73.9 us  [local(): pl.pallas_call(functools.partial(kernel, (nt, nd, chunks, kd), factor), o...]
where the time goes in v4:
time: 76.5 us; the launch traced here: 76.3 us
  Pallas kernels  75.7 us (99%)
    pallas_call x1, Pallas kernels, local(): pl.pallas_call(functools.partial(kernel, (nt, nd, chunks, kd), factor), o...  73.9 us
    pallas_call x1, Pallas kernels, local(): pl.pallas_call(write_out, out_shape=shapes, in_specs=[in_vmem] * 6, out_s...  1.75 us

profile of v4, /device:TPU:1, one launch (start us, length us, event | category | flops | bytes accessed | tf_op | source)
XLA Modules:
  0.0 76.3 jit_solution(7960368612142901036)
XLA Ops:
  0.6 73.9 %monarch.1 = (bf16[512,128]{1,0:T(8,128)(2,1)}, bf16[512,128]{1,0:T(8,128)(2,1)}, f32[1,32,128]{2,1,0:T(8,128)}, f32[4,8,128]{2,1,0:T(8,128)}, f32[4,8,128]{2,1,0:T(8,128)}, /*index=5*/f32[1,32,128]{2,1,0:T(8,128)}) custom-call(bf16[512,128]{1,0:T(8,128)(2,1)} %x_hbm.1, bf16[512,128]{1,0:T(8,128)(2,1)} %g_hbm.1, bf16[1,256,128]{2,1,0:T(8,128)(2,1)} %u1_hbm.1, ...), custom_call_target="tpu_custom_call" | custom-call | tf_op jit(solution)/shard_map/monarch/pallas_call | solution.py:361
  74.5 1.8 %write_out.1 = (bf16[512,128]{1,0:T(8,128)(2,1)}, bf16[512,128]{1,0:T(8,128)(2,1)}, f32[1,32,128]{2,1,0:T(8,128)}, f32[4,8,128]{2,1,0:T(8,128)}, f32[4,8,128]{2,1,0:T(8,128)}, /*index=5*/f32[1,32,128]{2,1,0:T(8,128)}) custom-call(bf16[512,128]{1,0:T(8,128)(2,1)} %get-tuple-element.12.refs_0_, bf16[512,128]{1,0:T(8,128)(2,1)} %get-tuple-element.13.refs_1_, ...), custom_call_target="tpu_custom_call" | custom-call | tf_op jit(solution)/shard_map/write_out/pallas_call | solution.py:406

commit v5 on v4

--- a/solution.py
+++ b/solution.py
@@ -48,10 +48,9 @@
     def tensor_peer(j):
         return lax.rem(me + nt + step * j, nt)
 
-    def greet_tensor(j, carry):
+    def greet_tensor(j):
         peer = tensor_peer(j)
         pl.semaphore_signal(barrier, inc=1, device_id={"tensor": peer}, device_id_type=MESH)
-        return carry
 
     def x_peer(j):
         return lax.rem(my_x + j, nx)
@@ -60,7 +59,8 @@
         pl.semaphore_signal(
             barrier, inc=1, device_id={"dp": other_half * nx + x_peer(j)}, device_id_type=MESH
         )
-    lax.fori_loop(1, nt, greet_tensor, 0)
+    for j in range(1, nt):
+        greet_tensor(j)
     for j in range(1, nx):
         pl.semaphore_signal(
             barrier, inc=1, device_id={"dp": my_half * nx + x_peer(j)}, device_id_type=MESH

time: 76.5 us -> 75.3 us (0.984)
  Pallas kernels: 75.7 us -> 74.3 us
    pallas_call x1, Pallas kernels: 73.9 us -> 72.5 us  [local(): pl.pallas_call(functools.partial(kernel, (nt, nd, chunks, kd), factor), o...]
where the time goes in v5:
time: 75.3 us; the launch traced here: 74.9 us
  Pallas kernels  74.3 us (99%)
    pallas_call x1, Pallas kernels, local(): pl.pallas_call(functools.partial(kernel, (nt, nd, chunks, kd), factor), o...  72.5 us
    pallas_call x1, Pallas kernels, local(): pl.pallas_call(write_out, out_shape=shapes, in_specs=[in_vmem] * 6, out_s...  1.75 us

profile of v5, /device:TPU:1, one launch (start us, length us, event | category | flops | bytes accessed | tf_op | source)
XLA Modules:
  0.0 74.9 jit_solution(16792229241727385228)
XLA Ops:
  0.6 72.5 %monarch.1 = (bf16[512,128]{1,0:T(8,128)(2,1)}, bf16[512,128]{1,0:T(8,128)(2,1)}, f32[1,32,128]{2,1,0:T(8,128)}, f32[4,8,128]{2,1,0:T(8,128)}, f32[4,8,128]{2,1,0:T(8,128)}, /*index=5*/f32[1,32,128]{2,1,0:T(8,128)}) custom-call(bf16[512,128]{1,0:T(8,128)(2,1)} %x_hbm.1, bf16[512,128]{1,0:T(8,128)(2,1)} %g_hbm.1, bf16[1,256,128]{2,1,0:T(8,128)(2,1)} %u1_hbm.1, ...), custom_call_target="tpu_custom_call" | custom-call | tf_op jit(solution)/shard_map/monarch/pallas_call | solution.py:361
  73.2 1.8 %write_out.1 = (bf16[512,128]{1,0:T(8,128)(2,1)}, bf16[512,128]{1,0:T(8,128)(2,1)}, f32[1,32,128]{2,1,0:T(8,128)}, f32[4,8,128]{2,1,0:T(8,128)}, f32[4,8,128]{2,1,0:T(8,128)}, /*index=5*/f32[1,32,128]{2,1,0:T(8,128)}) custom-call(bf16[512,128]{1,0:T(8,128)(2,1)} %get-tuple-element.12.refs_0_, bf16[512,128]{1,0:T(8,128)(2,1)} %get-tuple-element.13.refs_1_, ...), custom_call_target="tpu_custom_call" | custom-call | tf_op jit(solution)/shard_map/write_out/pallas_call | solution.py:406

commit v6 on v5

--- a/solution.py
+++ b/solution.py
@@ -81,7 +81,7 @@
         ).start()
 
         def one(j, carry):
-            peer = tensor_peer(j)
+            peer = lax.rem(me + j, nt) if which == 3 else tensor_peer(j)
             side = lax.rem(peer // (nt // 2) + run_half, 2) if which == 3 else 0
             pltpu.make_async_remote_copy(
                 src_ref=send.at[which, peer],

time: 75.3 us -> 73.5 us (0.976)
  Pallas kernels: 74.3 us -> 72.7 us
    pallas_call x1, Pallas kernels: 72.5 us -> 70.9 us  [local(): pl.pallas_call(functools.partial(kernel, (nt, nd, chunks, kd), factor), o...]
where the time goes in v6:
time: 73.5 us; the launch traced here: 73.3 us
  Pallas kernels  72.7 us (99%)
    pallas_call x1, Pallas kernels, local(): pl.pallas_call(functools.partial(kernel, (nt, nd, chunks, kd), factor), o...  70.9 us
    pallas_call x1, Pallas kernels, local(): pl.pallas_call(write_out, out_shape=shapes, in_specs=[in_vmem] * 6, out_s...  1.75 us

profile of v6, /device:TPU:1, one launch (start us, length us, event | category | flops | bytes accessed | tf_op | source)
XLA Modules:
  0.0 73.3 jit_solution(18251470484939967174)
XLA Ops:
  0.6 70.9 %monarch.1 = (bf16[512,128]{1,0:T(8,128)(2,1)}, bf16[512,128]{1,0:T(8,128)(2,1)}, f32[1,32,128]{2,1,0:T(8,128)}, f32[4,8,128]{2,1,0:T(8,128)}, f32[4,8,128]{2,1,0:T(8,128)}, /*index=5*/f32[1,32,128]{2,1,0:T(8,128)}) custom-call(bf16[512,128]{1,0:T(8,128)(2,1)} %x_hbm.1, bf16[512,128]{1,0:T(8,128)(2,1)} %g_hbm.1, bf16[1,256,128]{2,1,0:T(8,128)(2,1)} %u1_hbm.1, ...), custom_call_target="tpu_custom_call" | custom-call | tf_op jit(solution)/shard_map/monarch/pallas_call | solution.py:361
  71.6 1.8 %write_out.1 = (bf16[512,128]{1,0:T(8,128)(2,1)}, bf16[512,128]{1,0:T(8,128)(2,1)}, f32[1,32,128]{2,1,0:T(8,128)}, f32[4,8,128]{2,1,0:T(8,128)}, f32[4,8,128]{2,1,0:T(8,128)}, /*index=5*/f32[1,32,128]{2,1,0:T(8,128)}) custom-call(bf16[512,128]{1,0:T(8,128)(2,1)} %get-tuple-element.12.refs_0_, bf16[512,128]{1,0:T(8,128)(2,1)} %get-tuple-element.13.refs_1_, ...), custom_call_target="tpu_custom_call" | custom-call | tf_op jit(solution)/shard_map/write_out/pallas_call | solution.py:406

commit v7 on v6

--- a/solution.py
+++ b/solution.py
@@ -27,7 +27,7 @@
     x, g, u1, u2, d1, d2, out, gt, gsum,
     send, recv, wide, nk, bk, hid, slope, gpre,
     home, part, packed, landed, direct, half, half_packed, half_landed,
-    in_sem, out_sem, send_sem, recv_sem, psend_sem, precv_sem, hsend_sem, hrecv_sem,
+    in_sem, out_sem, send_sem, recv_sem, psend_sem, precv_sem, hsend_sem, hrecv_sem, ready,
 ):
     nt, nd, chunks, kd = sizes
     nx = nd // 2
@@ -42,30 +42,6 @@
     hidden_blocks = nt * kd
     tok = chunks * LANES
 
-    barrier = pltpu.get_barrier_semaphore()
-    step = jnp.where(me >= nt // 2, 1, -1)
-
-    def tensor_peer(j):
-        return lax.rem(me + nt + step * j, nt)
-
-    def greet_tensor(j):
-        peer = tensor_peer(j)
-        pl.semaphore_signal(barrier, inc=1, device_id={"tensor": peer}, device_id_type=MESH)
-
-    def x_peer(j):
-        return lax.rem(my_x + j, nx)
-
-    for j in range(nx):
-        pl.semaphore_signal(
-            barrier, inc=1, device_id={"dp": other_half * nx + x_peer(j)}, device_id_type=MESH
-        )
-    for j in range(1, nt):
-        greet_tensor(j)
-    for j in range(1, nx):
-        pl.semaphore_signal(
-            barrier, inc=1, device_id={"dp": my_half * nx + x_peer(j)}, device_id_type=MESH
-        )
-
     loads = [
         pltpu.make_async_copy(src, dst, in_sem.at[i])
         for i, (src, dst) in enumerate(
@@ -74,6 +50,37 @@
     ]
     for load in loads:
         load.start()
+
+    barrier = pltpu.get_barrier_semaphore()
+    step = jnp.where(me >= nt // 2, 1, -1)
+
+    def tensor_peer(j):
+        return lax.rem(me + nt + step * j, nt)
+
+    def greet_tensor(j):
+        peer = tensor_peer(j)
+        pl.semaphore_signal(barrier, inc=1, device_id={"tensor": peer}, device_id_type=MESH)
+
+    def x_peer(j):
+        return lax.rem(my_x + j, nx)
+
+    def tell_other_half(semaphore):
+        for j in range(nx):
+            pl.semaphore_signal(
+                semaphore,
+                inc=1,
+                device_id={"dp": other_half * nx + x_peer(j)},
+                device_id_type=MESH,
+            )
+
+    pl.when(my_half == 1)(lambda: tell_other_half(barrier))
+    for j in range(1, nt):
+        greet_tensor(j)
+    for j in range(1, nx):
+        pl.semaphore_signal(
+            barrier, inc=1, device_id={"dp": my_half * nx + x_peer(j)}, device_id_type=MESH
+        )
+
 
     def exchange(which):
         pltpu.make_async_copy(
@@ -167,7 +174,8 @@
     loads[0].wait()
     loads[1].wait()
     narrow_to_send(0, u1, x)
-    pl.semaphore_wait(barrier, nt - 1 + nd - 1)
+    pl.semaphore_wait(barrier, nt - 1 + nx - 1 + other_half * nx)
+    pl.when(my_half == 0)(lambda: tell_other_half(ready))
     exchange(0)
     loads[2].wait()
     loads[3].wait()
@@ -291,6 +299,7 @@
     leave(2, d2, x, out)
     store(out, out_hbm)
 
+    pl.when(my_half == 1)(lambda: pl.semaphore_wait(ready, nx))
     for side in range(2):
         arrived_side(side)
         unpack_side(side)
@@ -397,6 +406,7 @@
             pltpu.SemaphoreType.DMA((4,)),
             pltpu.SemaphoreType.DMA((3,)),
             pltpu.SemaphoreType.DMA((3,)),
+            pltpu.SemaphoreType.REGULAR,
         ],
         compiler_params=pltpu.CompilerParams(
             collective_id=0, has_side_effects=True, vmem_limit_bytes=63 * 1024 * 1024

time: 73.5 us -> 73.9 us (level)
  no operation moved by 1% of the time
where the time goes in v7:
time: 73.9 us; the launch traced here: 73.7 us
  Pallas kernels  73.1 us (99%)
    pallas_call x1, Pallas kernels, local(): pl.pallas_call(functools.partial(kernel, (nt, nd, chunks, kd), factor), o...  71.3 us
    pallas_call x1, Pallas kernels, local(): pl.pallas_call(write_out, out_shape=shapes, in_specs=[in_vmem] * 6, out_s...  1.75 us

profile of v7, /device:TPU:1, one launch (start us, length us, event | category | flops | bytes accessed | tf_op | source)
XLA Modules:
  0.0 73.7 jit_solution(448793245601660027)
XLA Ops:
  0.6 71.3 %monarch.1 = (bf16[512,128]{1,0:T(8,128)(2,1)}, bf16[512,128]{1,0:T(8,128)(2,1)}, f32[1,32,128]{2,1,0:T(8,128)}, f32[4,8,128]{2,1,0:T(8,128)}, f32[4,8,128]{2,1,0:T(8,128)}, /*index=5*/f32[1,32,128]{2,1,0:T(8,128)}) custom-call(bf16[512,128]{1,0:T(8,128)(2,1)} %x_hbm.1, bf16[512,128]{1,0:T(8,128)(2,1)} %g_hbm.1, bf16[1,256,128]{2,1,0:T(8,128)(2,1)} %u1_hbm.1, ...), custom_call_target="tpu_custom_call" | custom-call | tf_op jit(solution)/shard_map/monarch/pallas_call | solution.py:370
  71.9 1.8 %write_out.1 = (bf16[512,128]{1,0:T(8,128)(2,1)}, bf16[512,128]{1,0:T(8,128)(2,1)}, f32[1,32,128]{2,1,0:T(8,128)}, f32[4,8,128]{2,1,0:T(8,128)}, f32[4,8,128]{2,1,0:T(8,128)}, /*index=5*/f32[1,32,128]{2,1,0:T(8,128)}) custom-call(bf16[512,128]{1,0:T(8,128)(2,1)} %get-tuple-element.12.refs_0_, bf16[512,128]{1,0:T(8,128)(2,1)} %get-tuple-element.13.refs_1_, ...), custom_call_target="tpu_custom_call" | custom-call | tf_op jit(solution)/shard_map/write_out/pallas_call | solution.py:416
